TPU v7x, 32 devices: a whole 2x2x4 slice. The times are simulated.
32 devices in a mesh: ctx: 8 (over z, core), fsdp: 4 (over y, x).
Axes of the slice: x: 2, y: 2, z: 4, core: 2. Of those that a mesh axis runs over, the one named last changes fastest.
Arguments:
- hidden: bfloat16 [2, 4, 512, 2048], P(None, 'fsdp', 'ctx'), may hold values from -6 to 6
- cotangent: bfloat16 [2, 4, 512, 2048], P(None, 'fsdp', 'ctx'), may hold values from -6 to 6
- lengths: int32 [2, 4], P(None, 'fsdp'), may hold values from 128 to 512, as said below
- norm_gain: float32 [2048], replicated, may hold values from 0.5 to 1.5
- input_weight: bfloat16 [2048, 8512], P('fsdp'), may hold values from -0.125 to 0.125
- conv_w: float32 [4, 4352], replicated, may hold values from -3 to 3
- conv_b: float32 [4352], replicated, may hold values from -3 to 3
- dt_bias: float32 [64], replicated, may hold values from -4 to -2
- a_log: float32 [64], replicated, may hold values from -10 to -0.5
- d_skip: float32 [64], replicated, may hold values from 0.5 to 1.5
- gate_gain: float32 [4096], replicated, may hold values from 0.5 to 1.5
- output_weight: bfloat16 [4096, 2048], P('fsdp'), may hold values from -0.09375 to 0.09375
Outputs:
- out: bfloat16 [2, 4, 512, 2048], P(None, 'fsdp', 'ctx')
- d_hidden: float32 [2, 4, 512, 2048], P(None, 'fsdp', 'ctx')
- grad_norm_gain: float32 [2048], replicated
- grad_in_w: float32 [2048, 8512], P(('ctx', 'fsdp'))
- grad_conv_w: float32 [4, 4352], replicated
- grad_conv_b: float32 [4352], replicated
- grad_dt_bias: float32 [64], replicated
- grad_a_log: float32 [64], replicated
- grad_d_skip: float32 [64], replicated
- grad_gate_gain: float32 [4096], replicated
- grad_out_w: float32 [4096, 2048], P(('ctx', 'fsdp'))
Inputs may be any that keep to these rules, and one draw needn't show every extreme that they name: `lengths`: some sequence has all 512 slots live in every draw.
All inputs are finite; a program needn't handle non-finite values.
Results may differ from a plain program's by a relative error of at most 0.012.
The roundings to bfloat16 on the way count: a program that leaves them out, or rounds other values in their place, can miss the bound.
Values may be sent and summed in bfloat16 or wider, within the bound.
A program may use at most 384 MiB of HBM per device.

v0:
```python
import functools

import jax
import jax.numpy as jnp
from jax import lax
from jax.experimental import pallas as pl
from jax.experimental.pallas import tpu as pltpu
from jax.sharding import PartitionSpec as P

D = 2048
HEADS = 64
HEAD_DIM = 64
N_STATE = 128
CONV_K = 4
DI = 4096
CH = DI + 2 * N_STATE
LANES = 128
EPS = 1e-05
F32 = jnp.float32
BF16 = jnp.bfloat16
EXACT = lax.Precision.HIGHEST
VMEM_LIMIT = 63 * 1024 * 1024


def dot(a, b, ca=1, cb=0):
    return lax.dot_general(
        a.astype(BF16), b.astype(BF16), (((ca,), (cb,)), ((), ())), preferred_element_type=F32
    )


def dot_exact(a, b):
    return lax.dot_general(
        a, b, (((1,), (0,)), ((), ())), precision=EXACT, preferred_element_type=F32
    )


def to_lanes(per_head, width):
    q = per_head.shape[0]
    low = lax.broadcasted_iota(jnp.int32, (q, LANES), 1) < HEAD_DIM
    pairs = []
    for j in range(width // LANES):
        first = jnp.broadcast_to(per_head[:, 2 * j : 2 * j + 1], (q, LANES))
        second = jnp.broadcast_to(per_head[:, 2 * j + 1 : 2 * j + 2], (q, LANES))
        pairs.append(jnp.where(low, first, second))
    return jnp.concatenate(pairs, axis=1)


def head_sum_matrix(width):
    channel = lax.broadcasted_iota(jnp.int32, (width, LANES), 0) // HEAD_DIM
    return (channel == lax.broadcasted_iota(jnp.int32, (width, LANES), 1)).astype(F32)


def split_heads(pair):
    low = lax.broadcasted_iota(jnp.int32, pair.shape, 1) < HEAD_DIM
    zero = jnp.zeros_like(pair)
    return jnp.concatenate([jnp.where(low, pair, zero), jnp.where(low, zero, pair)], axis=0)


def triangle(q, lower):
    rows = lax.broadcasted_iota(jnp.int32, (q, q), 0)
    cols = lax.broadcasted_iota(jnp.int32, (q, q), 1)
    return (rows >= cols) if lower else (rows <= cols)


def softplus(z):
    return jnp.maximum(z, 0.0) + jnp.log(1.0 + jnp.exp(-jnp.abs(z)))


def live_column(lengths_ref, s, chunk, q):
    slots = chunk * q + lax.broadcasted_iota(jnp.int32, (q, LANES), 0)
    return (slots < lengths_ref[s]).astype(F32)


def decays(dt_raw, bias, rate, live):
    q = dt_raw.shape[0]
    z = dt_raw + bias
    step = softplus(z) * live
    cum = dot_exact(triangle(q, True).astype(F32), step * rate)
    return z, step, cum


def head_pick(cw, span, me_c):
    mine, apart, each = cw // HEAD_DIM, HEADS // span, cw // HEAD_DIM // span
    lane = lax.broadcasted_iota(jnp.int32, (HEADS, LANES), 1)
    head = (lane // each) * apart + me_c * each + lax.rem(lane, each)
    row = lax.broadcasted_iota(jnp.int32, (HEADS, LANES), 0)
    return jnp.logical_and(row == head, lane < mine).astype(F32)


def forward_chunk(cw, chunk, s, lengths, proj, pick, conv_w, heads_par, chan_par, mixed_out, state_out, window, state):
    per = 2 if proj.shape[0] % 2 == 0 else 1
    length = proj.shape[2]
    q = per * length
    cc = cw + 2 * N_STATE
    causal = triangle(q, True)
    at = pl.ds(chunk * per, per)
    rows = proj[at, s].reshape(q, proj.shape[3])
    window[s, 8 : 8 + q, :] = rows[:, cw : cw + cc].astype(F32)
    pre = conv_w[CONV_K : CONV_K + 1, :] + conv_w[0:1, :] * window[s, 5 : 5 + q, :]
    for k in range(1, CONV_K):
        pre = pre + conv_w[k : k + 1, :] * window[s, 5 + k : 5 + k + q, :]
    window[s, 0:8, :] = window[s, q : q + 8, :]
    act = pre * jax.nn.sigmoid(pre)
    x = act[:, :cw]
    b = act[:, cw : cw + N_STATE]
    c = act[:, cw + N_STATE :]
    live = live_column(lengths, s, chunk, q)
    _, step, cum = decays(
        dot(rows[:, cw + cc :], pick[...]), heads_par[0:1, :], heads_par[1:2, :], live
    )
    cum_t = cum.T
    last = cum[q - 1 : q, :]
    u = x * to_lanes(step, cw)
    gram = dot(c, b, 1, 1)
    within = []
    for j in range(cw // LANES):
        kernels = []
        for h in (2 * j, 2 * j + 1):
            spread = jnp.where(causal, cum[:, h : h + 1] - cum_t[h : h + 1, :], -1e30)
            kernels.append((gram * jnp.exp(spread)).astype(BF16))
        both = jnp.concatenate(kernels, axis=1)
        within.append(dot(both, split_heads(u[:, j * LANES : (j + 1) * LANES])))
    before = state[s]
    state_out[chunk, s] = before.astype(BF16)
    mixed_out[chunk, s] = (
        jnp.concatenate(within, axis=1)
        + dot(c, before) * to_lanes(jnp.exp(cum), cw)
        + chan_par[0:1, :] * x
    )
    left = to_lanes(jnp.exp(last - cum), cw)
    state[s] = before * to_lanes(jnp.exp(last), cw) + dot(b, left * u, 0, 0)


def slot_columns(scales, chunk, s, row, cw):
    q = scales.shape[3]
    column = jnp.broadcast_to(scales[chunk, s, row : row + 1, :], (LANES, q)).T
    return jnp.concatenate([column] * (cw // LANES), axis=1)


def gated_chunk(cw, chunk, s, proj, scales, chan_par, mixed, gated):
    per = proj.shape[0] // mixed.shape[0]
    length = proj.shape[2]
    q = per * length
    at = pl.ds(chunk * per, per)
    gate = proj[at, s, :, :cw].reshape(q, cw).astype(F32)
    g = mixed[chunk, s] * gate * jax.nn.sigmoid(gate)
    normal = g * slot_columns(scales, chunk, s, 0, cw) * chan_par[1:2, :]
    gated[at, s] = normal.astype(BF16).reshape(per, length, cw)


def gate_chunk(cw, chunk, s, proj, scales, chan_par, gg, mixed, dchan):
    per = proj.shape[0] // mixed.shape[0]
    length = proj.shape[2]
    q = per * length
    at = pl.ds(chunk * per, per)
    gate = proj[at, s, :, :cw].reshape(q, cw).astype(F32)
    scale, pull = (slot_columns(scales, chunk, s, i, cw) for i in range(2))
    grad = gg[at, s].reshape(q, cw)
    sig = jax.nn.sigmoid(gate)
    silu = gate * sig
    m = mixed[chunk, s]
    g = m * silu
    gain = chan_par[1:2, :]
    dchan[1:2, :] += jnp.sum(grad * g * scale, axis=0, keepdims=True)
    dg = scale * (grad * gain - g * pull)
    gg[at, s] = (dg * silu).reshape(per, length, cw)
    dgate = dg * m * (sig * (1.0 + gate * (1.0 - sig)))
    proj[at, s, :, :cw] = dgate.astype(BF16).reshape(per, length, cw)


def backward_chunk(
    cw, chunk, s, lengths, proj, pick, conv_w, heads_par, chan_par, gm_in, mixed_in, state_in,
    dconv, dheads, dchan, window, ahead, state_grad,
):
    per = proj.shape[0] // mixed_in.shape[0]
    length = proj.shape[2]
    q = per * length
    cc = cw + 2 * N_STATE
    causal = triangle(q, True)
    sums = head_sum_matrix(cw)
    at = pl.ds(chunk * per, per)
    rows = proj[at, s, :, cw:].reshape(q, proj.shape[3] - cw)
    conv_in = rows[:, :cc].astype(F32)
    mixed = mixed_in[chunk, s]
    gm = gm_in[at, s].reshape(q, cw)
    if chunk:
        tail = proj[chunk * per - 1, s, length - 16 :, cw : cw + cc].astype(F32)
        window[s, 0:8, :] = tail[8:16]
    else:
        window[s, 0:8, :] = jnp.zeros((8, cc), F32)
    window[s, 8 : 8 + q, :] = conv_in
    pre = conv_w[CONV_K : CONV_K + 1, :] + conv_w[0:1, :] * window[s, 5 : 5 + q, :]
    for k in range(1, CONV_K):
        pre = pre + conv_w[k : k + 1, :] * window[s, 5 + k : 5 + k + q, :]
    sig_pre = jax.nn.sigmoid(pre)
    act = pre * sig_pre
    x = act[:, :cw]
    b = act[:, cw : cw + N_STATE]
    c = act[:, cw + N_STATE :]
    live = live_column(lengths, s, chunk, q)
    z, step, cum = decays(dot(rows[:, cc:], pick[...]), heads_par[0:1, :], heads_par[1:2, :], live)
    cum_t = cum.T
    last = cum[q - 1 : q, :]
    step_l = to_lanes(step, cw)
    u = x * step_l
    gram = dot(c, b, 1, 1)
    dchan[0:1, :] += jnp.sum(gm * x, axis=0, keepdims=True)
    du = []
    dgram = jnp.zeros((q, q), F32)
    for j in range(cw // LANES):
        lanes = slice(j * LANES, (j + 1) * LANES)
        dkernels = dot(gm[:, lanes], split_heads(u[:, lanes]), 1, 1)
        kernels = []
        for i in range(2):
            h = 2 * j + i
            spread = jnp.where(causal, cum[:, h : h + 1] - cum_t[h : h + 1, :], -1e30)
            decay = jnp.exp(spread)
            dgram = dgram + dkernels[:, i * q : (i + 1) * q] * decay
            kernels.append((gram * decay).astype(BF16))
        both = jnp.concatenate(kernels, axis=0)
        du.append(dot(both, split_heads(gm[:, lanes]), 0, 0))
    before = state_in[chunk, s].astype(F32)
    after_grad = state_grad[s]
    v = gm * to_lanes(jnp.exp(cum), cw)
    left = to_lanes(jnp.exp(last - cum), cw)
    du_state = left * dot(b, after_grad)
    du = jnp.concatenate(du, axis=1) + du_state
    dc = dot(dgram, b) + dot(v, before, 1, 1)
    db = dot(dgram, c, 0, 0) + dot(left * u, after_grad, 1, 1)
    end = to_lanes(jnp.exp(last), cw)
    extra = jnp.sum(u * du_state, axis=0, keepdims=True) + end * jnp.sum(
        after_grad * before, axis=0, keepdims=True
    )
    state_grad[s] = end * after_grad + dot(c, v, 0, 0)
    last_row = (lax.broadcasted_iota(jnp.int32, (q, LANES), 0) == q - 1).astype(F32)
    dcum = dot_exact(gm * (mixed - chan_par[0:1, :] * x) - u * du, sums) + last_row * dot_exact(
        jnp.broadcast_to(extra, (8, cw)), sums
    )[0:1, :]
    dlog = dot_exact(triangle(q, False).astype(F32), dcum)
    rate = heads_par[1:2, :]
    dstep = dot_exact(x * du, sums) + dlog * rate
    dheads[1:2, :] += jnp.sum(dlog * step * rate, axis=0, keepdims=True)
    dz = dstep * live * jax.nn.sigmoid(z)
    dheads[0:1, :] += jnp.sum(dz, axis=0, keepdims=True)
    dx = step_l * du + chan_par[0:1, :] * gm
    dpre = jnp.concatenate([dx, db, dc], axis=1) * (sig_pre * (1.0 + pre * (1.0 - sig_pre)))
    ahead[s, 0:q, :] = dpre
    dconv_in = jnp.zeros((q, cc), F32)
    for k in range(CONV_K):
        first = CONV_K - 1 - k
        moved = ahead[s, first : first + q, :]
        dconv_in = dconv_in + conv_w[k : k + 1, :] * moved
        dconv[k : k + 1, :] += jnp.sum(conv_in * moved, axis=0, keepdims=True)
    dconv[CONV_K : CONV_K + 1, :] += jnp.sum(dpre, axis=0, keepdims=True)
    ahead[s, q : q + 8, :] = ahead[s, 0:8, :]
    proj[at, s, :, cw : cw + cc] = dconv_in.astype(BF16).reshape(per, length, cc)
    dz = dot(dz, pick[...], 1, 1).astype(BF16)
    proj[at, s, :, cw + cc :] = dz.reshape(per, length, HEADS)


def column_tiles(n, body, size=256):
    if n <= size:
        body(0, n)
        return

    def one(j, _):
        body(pl.multiple_of(j * size, size), size)
        return 0

    lax.fori_loop(0, n // size, one, 0)


MESH = pl.DeviceIdType.MESH


class push:
    def __init__(self, src, dst, send_sem, recv_sem, device):
        self.args = (src, dst, send_sem, recv_sem, device, MESH)

    def start(self):
        pltpu.make_async_remote_copy(*self.args).start()

    def wait_send(self):
        pltpu.make_async_remote_copy(*self.args).wait_send()

    def wait_recv(self):
        pltpu.make_async_remote_copy(*self.args).wait_recv()

    def wait(self):
        self.wait_send()
        self.wait_recv()


def greet(devices_and_tests):
    return signal_all(pltpu.get_barrier_semaphore(), devices_and_tests)


def signal_all(barrier, devices_and_tests):
    count = 0
    for device, there in devices_and_tests:
        if there is None:
            pl.semaphore_signal(barrier, inc=1, device_id=device, device_id_type=MESH)
            count = count + 1
        else:
            @pl.when(there)
            def _():
                pl.semaphore_signal(barrier, inc=1, device_id=device, device_id_type=MESH)

            count = count + there.astype(jnp.int32)
    return lambda: pl.semaphore_wait(barrier, count)


def line_of(nc):
    me = lax.axis_index("ctx")
    return nc // 2, me // 2, lax.rem(me, 2)


def square_partners():
    me = lax.axis_index("fsdp")
    high, low = me // 2, lax.rem(me, 2)
    return me, high * 2 + (1 - low), (1 - high) * 2 + low


class LineGather:
    def __init__(self, nc, every, sems):
        self.nz, self.z, self.k = line_of(nc)
        self.every = every
        self.up, self.down, self.side, self.got, self.got_side = sems

    def slot(self, place):
        return self.every.at[2 * place + self.k]

    def copies(self, d, below):
        z, k = self.z, self.k
        origin = z - d if below else z + d
        to = z + 1 if below else z - 1
        on = push(
            self.slot(origin), self.slot(origin), (self.up if below else self.down).at[d],
            self.got.at[origin], {"ctx": 2 * to + k},
        )
        side = push(
            self.slot(origin), self.slot(origin), self.side.at[origin], self.got_side.at[origin],
            {"ctx": 2 * z + 1 - k},
        )
        there = origin >= 0 if below else origin <= self.nz - 1
        further = to <= self.nz - 1 if below else to >= 0
        return on, side, there, further

    def begin(self):
        for below in (True, False):
            on, side, _, further = self.copies(0, below)
            pl.when(further)(on.start)
        side.start()

    def step(self, d):
        for below in (True, False):
            on, side, there, further = self.copies(d, below)

            @pl.when(there)
            def _():
                on.wait_recv()
                pl.when(further)(on.start)
                side.start()

    def sides(self, least, most):
        for place in range(self.nz):
            arrived = self.every.at[2 * place + 1 - self.k]
            apart = jnp.abs(place - self.z)
            pl.when(jnp.logical_and(apart >= least, apart <= most))(
                push(
                    arrived, arrived, self.side.at[place], self.got_side.at[place],
                    {"ctx": 2 * self.z + 1 - self.k},
                ).wait_recv
            )

    def end(self):
        for place in range(self.nz):
            arrived = self.every.at[2 * place + 1 - self.k]
            push(
                arrived, arrived, self.side.at[place], self.got_side.at[place],
                {"ctx": 2 * self.z + 1 - self.k},
            ).wait_send()
        for d in range(self.nz - 1):
            for below in (True, False):
                on, _, there, further = self.copies(d, below)
                pl.when(jnp.logical_and(there, further))(on.wait_send)


class SquareGather:
    def __init__(self, nf, every, sems):
        self.nf, self.every = nf, every
        self.send, self.got = sems
        self.half = every.shape[1] // 2

    def peers(self):
        me = lax.axis_index("fsdp")
        if self.nf == 4:
            _, fx, fy = square_partners()
            return [(fx, fx), (fy, fy)]
        return [
            (lax.rem(me + j, self.nf), lax.rem(me + self.nf - j, self.nf))
            for j in range(1, self.nf)
        ]

    def first(self):
        me = lax.axis_index("fsdp")
        for j, (to, frm) in enumerate(self.peers()):
            args = (self.send.at[j], self.got.at[j], {"fsdp": to})
            mine, theirs = self.every.at[me], self.every.at[frm]
            yield push(mine, mine, *args), push(theirs, theirs, *args)

    def second(self):
        me, fx, fy = square_partners()
        pairs = []
        for j, (via, to) in enumerate(((fx, fy), (fy, fx))):
            rows = pl.ds(j * self.half, self.half)
            args = (self.send.at[2 + j], self.got.at[2 + j], {"fsdp": to})
            there, here = self.every.at[via, rows], self.every.at[3 - me, rows]
            pairs.append((push(there, there, *args), push(here, here, *args)))
        return pairs

    def begin(self):
        for out, _ in self.first():
            out.start()

    def step(self):
        for j, (_, arrived) in enumerate(self.first()):
            arrived.wait_recv()
            if self.nf == 4:
                self.second()[j][0].start()

    def far(self):
        if self.nf == 4:
            for _, arrived in self.second():
                arrived.wait_recv()

    def end(self):
        for out, _ in self.first():
            out.wait_send()
        if self.nf == 4:
            for out, _ in self.second():
                out.wait_send()


class ChipGather:
    def __init__(self, nf, every, sems):
        self.nf, self.every = nf, every
        me = lax.axis_index("ctx")
        self.core, self.other = lax.rem(me, 2), {"ctx": me + 1 - 2 * lax.rem(me, 2)}
        self.half = every.shape[1] // 2
        mine = every.at[:, pl.ds(pl.multiple_of(self.core * self.half, 16), self.half)]
        self.square = SquareGather(nf, mine, sems[:2])
        self.send, self.got = sems[2:]

    def side(self, f, core):
        part = self.every.at[f, pl.ds(pl.multiple_of(core * self.half, 16), self.half)]
        return push(part, part, self.send.at[f], self.got.at[f], self.other)

    def near(self):
        return [frm for _, frm in self.square.peers()]

    def begin(self):
        self.square.begin()

    def step(self):
        self.square.step()
        for f in self.near():
            self.side(f, self.core).start()

    def sides(self):
        for f in self.near():
            self.side(f, 1 - self.core).wait_recv()

    def far(self):
        self.square.far()
        if self.nf == 4:
            f = 3 - lax.axis_index("fsdp")
            self.side(f, self.core).start()
            self.side(f, 1 - self.core).wait_recv()

    def end(self):
        self.square.end()
        for f in self.near():
            self.side(f, self.core).wait_send()
        if self.nf == 4:
            self.side(3 - lax.axis_index("fsdp"), self.core).wait_send()


class SquareSpread:
    def __init__(self, nf, source, every, sems):
        self.nf, self.every = nf, every
        self.send, self.got = sems
        self.mine = lax.axis_index("fsdp") == source

    def copies(self):
        me = lax.axis_index("fsdp")
        return [
            push(
                self.every, self.every, self.send.at[j], self.got.at[0],
                {"fsdp": lax.rem(me + j, self.nf)},
            )
            for j in range(1, self.nf)
        ]

    def begin(self):
        for out in self.copies():
            pl.when(self.mine)(out.start)

    def step(self):
        pass

    def far(self):
        if self.nf > 1:
            pl.when(jnp.logical_not(self.mine))(self.copies()[0].wait_recv)

    def end(self):
        for out in self.copies():
            pl.when(self.mine)(out.wait_send)


class Exchange:
    def __init__(self, axis, n, own, every, sems):
        self.axis, self.n, self.own, self.every = axis, n, own, every
        self.send, self.got = sems

    def copies(self):
        me = lax.axis_index(self.axis)
        for j in range(1, self.n):
            to, frm = lax.rem(me + j, self.n), lax.rem(me + self.n - j, self.n)
            args = (self.send.at[j], self.got.at[j], {self.axis: to})
            yield push(self.own, self.every.at[me], *args), push(self.own, self.every.at[frm], *args)

    def begin(self):
        self.every[lax.axis_index(self.axis)] = self.own[...]
        for out, _ in self.copies():
            out.start()

    def wait(self):
        for out, arrived in self.copies():
            arrived.wait_recv()
            out.wait_send()

    def total(self):
        result = self.every[0]
        for i in range(1, self.n):
            result = result + self.every[i]
        return result


def front_kernel(
    nc, nf, cw, span, lengths, hidden, cot, in_w, out_w, norm_gain, conv_w, conv_b, heads_in, gate_gain,
    normed_out, cot_out, main_out, tail_out, gated_out, proj_out, gg_out, mixed_out, states_out, branch_out,
    scales, conv_par, heads_par, chan_par, pick,
    normed_t, cot_v, main_v, tail_v, gated_t, proj, gg, mixed, states, branch, rows_v, normed_v, acc, gated,
    window, state, stats, stats_held, more, more_held,
    line_sems, main_sems, tail_sems, rows_sems, stat_sems, load_sems, keep_sems,
):
    nz, z, k = line_of(nc)
    me_c, me_f = lax.axis_index("ctx"), lax.axis_index("fsdp")
    wide, apart = cw // span, DI // span
    depth = in_w.shape[1]
    seqs, length = proj.shape[1], proj.shape[2]
    per = 2 if nc % 2 == 0 else 1
    q, chunks = per * length, nc // per

    found = [({"ctx": lax.rem(me_c + j, nc)}, None) for j in range(1, nc)]
    found += [({"fsdp": lax.rem(me_f + j, nf)}, None) for j in range(1, nf)]
    met = greet(found)

    loads = []

    def load(src, dst):
        copy = pltpu.make_async_copy(src, dst, load_sems.at[len(loads)])
        copy.start()
        loads.append(copy)

    for part in range(2):
        for i in range(span):
            start = pl.multiple_of(part * DI + i * apart + wide * me_c, LANES)
            load(in_w.at[pl.ds(start, wide)], main_v.at[me_f, pl.ds(part * cw + i * wide, wide)])
    load(in_w.at[pl.ds(2 * DI, tail_v.shape[1])], tail_v.at[me_f])
    weight_loads = len(loads)
    load(cot, cot_v.at[me_c])
    if span > 1:
        load(out_w.at[pl.ds(pl.multiple_of(wide * me_c, 16), wide)], rows_v.at[me_f])
    else:
        lap = out_w.shape[0] // cw
        held = me_f == me_c // lap
        rows_load = pltpu.make_async_copy(
            out_w.at[pl.ds(pl.multiple_of(cw * lax.rem(me_c, lap), 16), cw)], rows_v.at[0],
            load_sems.at[len(loads)],
        )
        pl.when(held)(rows_load.start)

    def norm(i, _):
        at = pl.ds(pl.multiple_of(i * 16, 16), 16)
        src = hidden[at].astype(F32)
        mean = jnp.mean(src * src, axis=1, keepdims=True)
        normed_v[me_c, at] = (src * lax.rsqrt(mean + EPS) * norm_gain[...]).astype(BF16)
        return 0

    lax.fori_loop(0, hidden.shape[0] // 16, norm, 0)

    line = lambda i, every: LineGather(nc, every, [line_sems.at[i, j] for j in range(5)])
    normed_line, cot_line = line(0, normed_v), line(1, cot_v)
    main = SquareGather(nf, main_v, (main_sems.at[0], main_sems.at[1]))
    tails = ChipGather(nf, tail_v, [tail_sems.at[i] for i in range(4)])
    if span > 1:
        rows = SquareGather(nf, rows_v, (rows_sems.at[0], rows_sems.at[1]))
    else:
        rows = SquareSpread(nf, me_c // lap, rows_v.at[0], (rows_sems.at[0], rows_sems.at[1]))
    kept = []

    def keep(src, dst):
        copy = pltpu.make_async_copy(src, dst, keep_sems.at[len(kept)])
        copy.start()
        kept.append(copy)

    for copy in loads[:weight_loads]:
        copy.wait()
    met()
    main.begin()
    normed_line.begin()
    tails.begin()

    pick[...] = head_pick(cw, span, me_c)
    conv_par[...] = jnp.zeros_like(conv_par)
    chan_par[...] = jnp.zeros_like(chan_par)
    for i in range(span):
        here = pl.ds(i * wide, wide)
        there = pl.ds(pl.multiple_of(i * apart + wide * me_c, LANES), wide)
        conv_par[0:CONV_K, here] = conv_w[:, there]
        conv_par[CONV_K : CONV_K + 1, here] = conv_b[:, there]
        chan_par[1:2, here] = gate_gain[:, there]
    conv_par[0:CONV_K, cw:] = conv_w[:, DI:CH]
    conv_par[CONV_K : CONV_K + 1, cw:] = conv_b[:, DI:CH]
    picked = dot_exact(heads_in[...], pick[...])
    heads_par[0:1, :] = picked[0:1, :]
    heads_par[1:2, :] = -jnp.exp(picked[1:2, :])
    heads_par[2:8, :] = jnp.zeros((6, LANES), F32)
    chan_par[0:1, :] = to_lanes(picked[2:3, :], cw)
    window[...] = jnp.zeros_like(window)
    state[...] = jnp.zeros_like(state)

    for copy in loads[weight_loads:]:
        copy.wait()
    if span == 1:
        pl.when(held)(rows_load.wait)
    slots = nc * normed_v.shape[1]

    def project(depths, first, last):
        def part(weights, base):
            def body(start, size):
                sums = None
                for f in depths:
                    a = normed_v[:, :, pl.ds(pl.multiple_of(f * depth, LANES), depth)]
                    term = dot(a.reshape(slots, depth), weights[f, pl.ds(start, size)], 1, 1)
                    sums = term if sums is None else sums + term
                here = pl.ds(base + start, size)
                if not first:
                    sums = sums + acc[:, here]
                if last:
                    proj[:, :, :, here] = sums.astype(BF16).reshape(proj.shape[:3] + (size,))
                else:
                    acc[:, here] = sums

            return body

        column_tiles(2 * cw, part(main_v, 0))
        column_tiles(tail_v.shape[1], part(tail_v, 2 * cw), tail_v.shape[1])

    for d in range(1, min(nz, 3)):
        normed_line.step(d)
    cot_line.begin()
    main.step()
    tails.step()
    for d in range(3, nz):
        normed_line.step(d)
    normed_line.sides(0, nz)
    tails.sides()
    if nf == 4:
        _, fx, fy = square_partners()
        project([me_f, fx, fy], True, False)
    if nz > 1:
        cot_line.step(1)
    main.far()
    tails.far()
    rows.begin()
    if nf == 4:
        project([3 - me_f], False, True)
    else:
        for j in range(nf):
            project([lax.rem(me_f + j, nf)], j == 0, j == nf - 1)
    keep(main_v, main_out)
    keep(tail_v, tail_out)
    keep(proj, proj_out)

    def across(a):
        total = a[:, :LANES]
        for j in range(1, cw // LANES):
            total = total + a[:, j * LANES : (j + 1) * LANES]
        return jnp.sum(total.T, axis=0, keepdims=True)

    def before_norm(chunk, s):
        at = pl.ds(chunk * per, per)
        gate = proj[at, s, :, :cw].reshape(q, cw).astype(F32)
        return at, mixed[chunk, s] * gate * jax.nn.sigmoid(gate)

    for chunk in range(chunks):
        for s in range(seqs):
            forward_chunk(
                cw, chunk, s, lengths, proj, pick, conv_par, heads_par, chan_par, mixed, states,
                window, state,
            )
            _, g = before_norm(chunk, s)
            row = chunk * seqs + s
            stats[row : row + 1, :] = across(g * g)
        if chunk == chunks // 2 - 1:
            rows.step()
    squares = Exchange("ctx", nc, stats, stats_held, (stat_sems.at[0, 0], stat_sems.at[0, 1]))
    squares.begin()
    keep(mixed, mixed_out)
    keep(states, states_out)
    for d in range(2, nz - 1):
        cot_line.step(d)
    mine = normed_v.shape[1]

    def turn(c, _):
        normed_t[:, pl.ds(pl.multiple_of(c * mine, LANES), mine)] = normed_v[c].T
        return 0

    lax.fori_loop(0, nc, turn, 0)
    keep(normed_t, normed_out)
    squares.wait()
    totals = squares.total() * (1.0 / DI)
    for chunk in range(chunks):
        for s in range(seqs):
            row = chunk * seqs + s
            scales[chunk, s, 0:1, :] = lax.rsqrt(totals[row : row + 1, :] + EPS)
            gated_chunk(cw, chunk, s, proj, scales, chan_par, mixed, gated)
    rows.far()

    def branch_tile(start, size):
        part = dot(gated[...].reshape(slots, cw), rows_v[:, :, pl.ds(start, size)].reshape(cw, size))
        part = part.astype(BF16).reshape(nc, seqs, length, size)
        for s in range(seqs):
            branch[s, :, :, pl.ds(start, size)] = part[:, s]

    column_tiles(D, branch_tile)
    keep(branch, branch_out)
    gated_t[...] = gated[...].reshape(slots, cw).T
    keep(gated_t, gated_out)

    if nz > 2:
        cot_line.step(nz - 1)
    cot_line.sides(0, nz)
    keep(cot_v, cot_out)
    cots = cot_v[...].reshape(slots, D)
    weights = rows_v[...].reshape(cw, D)
    half = min(cw, 256)
    for i in range(cw // half):
        gg[:, :, :, i * half : (i + 1) * half] = dot(
            cots, weights[i * half : (i + 1) * half], 1, 1
        ).reshape(gg.shape[:3] + (half,))
    keep(gg, gg_out)
    for chunk in range(chunks):
        for s in range(seqs):
            at, g = before_norm(chunk, s)
            row = chunk * seqs + s
            more[row : row + 1, :] = across(gg[at, s].reshape(q, cw) * chan_par[1:2, :] * g)
    pulls = Exchange("ctx", nc, more, more_held, (stat_sems.at[1, 0], stat_sems.at[1, 1]))
    pulls.begin()
    pulls.wait()
    totals = pulls.total() * (1.0 / DI)
    for chunk in range(chunks):
        for s in range(seqs):
            row = chunk * seqs + s
            scale = scales[chunk, s, 0:1, :]
            scales[chunk, s, 1:2, :] = scale * scale * totals[row : row + 1, :]
            scales[chunk, s, 2:8, :] = jnp.zeros((6, q), F32)
    for part in (main, tails, rows, normed_line, cot_line):
        part.end()
    for copy in kept:
        copy.wait()


def call_front(nc, nf, cw, span, lengths, hidden, cot, in_w, out_w, norm_gain, conv_w, conv_b, heads_in, gate_gain):
    nz = nc // 2
    mine = hidden.shape[0]
    seqs = lengths.shape[0]
    length = mine // seqs
    per = 2 if nc % 2 == 0 else 1
    q, chunks, cc = per * length, nc // per, cw + 2 * N_STATE
    depth, wide, ends = in_w.shape[1], cw // span, in_w.shape[0] - 2 * DI
    cols = 2 * cw + ends
    vmem = pl.BlockSpec(memory_space=pltpu.VMEM)
    anywhere = pl.BlockSpec(memory_space=pl.ANY)
    dma = pltpu.SemaphoreType.DMA
    big = [
        ((D, nc * mine), BF16),
        ((nc, mine, D), BF16),
        ((nf, 2 * cw, depth), BF16),
        ((nf, ends, depth), BF16),
        ((cw, nc * mine), BF16),
        ((nc, seqs, length, cols), BF16),
        ((nc, seqs, length, cw), F32),
        ((chunks, seqs, q, cw), F32),
        ((chunks, seqs, N_STATE, cw), BF16),
        ((seqs, nc, length, D), BF16),
    ]
    small = [
        ((chunks, seqs, 8, q), F32),
        ((8, cc), F32),
        ((8, LANES), F32),
        ((8, cw), F32),
        ((HEADS, LANES), F32),
    ]
    held = big + [
        ((span, wide, D), BF16),
        ((nc, mine, D), BF16),
        ((nc * mine, cols), F32),
        ((nc, seqs, length, cw), BF16),
        ((seqs, q + 8, cc), F32),
        ((seqs, N_STATE, cw), F32),
    ]
    held += [((chunks * seqs, q), F32), ((nc, chunks * seqs, q), F32)] * 2
    places = max(nf, 4)
    return pl.pallas_call(
        functools.partial(front_kernel, nc, nf, cw, span),
        in_specs=[pl.BlockSpec(memory_space=pltpu.SMEM), vmem, vmem, anywhere, anywhere]
        + [vmem] * 5,
        out_specs=[anywhere] * len(big) + [vmem] * len(small),
        out_shape=[jax.ShapeDtypeStruct(*a) for a in big + small],
        scratch_shapes=[pltpu.VMEM(*a) for a in held]
        + [
            dma((2, 5, nz)),
            dma((2, places)),
            dma((4, places)),
            dma((2, places)),
            dma((2, 2, nc)),
            dma((2 * span + 3,)),
            dma((10,)),
        ],
        compiler_params=pltpu.CompilerParams(
            collective_id=0, has_side_effects=True, vmem_limit_bytes=VMEM_LIMIT
        ),
        name="front",
    )(lengths, hidden, cot, in_w, out_w, norm_gain, conv_w, conv_b, heads_in, gate_gain)


def add_rows(into, other, rows=16):
    def body(i, _):
        at = pl.ds(pl.multiple_of(i * rows, rows), rows)
        into[at] = (into[at].astype(F32) + other[at].astype(F32)).astype(into.dtype)
        return 0

    lax.fori_loop(0, into.shape[0] // rows, body, 0)


class LineReduce:
    def __init__(self, nc, parts, acc, landed, sems):
        self.nz, self.z, self.k = line_of(nc)
        self.parts, self.acc, self.landed = parts, acc, landed
        self.side, self.got_side, self.send, self.got = sems

    def to_side(self, place):
        other = {"ctx": 2 * self.z + 1 - self.k}
        return push(
            self.parts.at[2 * place + 1 - self.k], self.acc.at[place], self.side.at[place],
            self.got_side.at[place], other,
        )

    def begin(self):
        for place in range(self.nz):
            self.to_side(place).start()

    def merge(self):
        for place in range(self.nz):
            self.to_side(place).wait_recv()
            add_rows(self.acc.at[place], self.parts.at[2 * place + self.k])

    def along(self, place, up):
        way = 0 if up else 1
        slot = place if up else jnp.where(place == self.z - 1, self.nz, place)
        return push(
            self.acc.at[place], self.landed.at[slot], self.send.at[way, place],
            self.got.at[way, place], {"ctx": 2 * (self.z + (1 if up else -1)) + self.k},
        )

    def arrive(self, place, up, into, slot=None):
        self.along(place, up).wait_recv()
        add_rows(into, self.landed.at[place if slot is None else slot])

    def step(self, tick):
        z, nz = self.z, self.nz
        for place in range(nz):
            for up in (True, False):
                at = tick - (nz - 1 - place) if up else nz - 1 + place - tick
                if not (0 <= at < place if up else place < at <= nz - 1):
                    continue
                first, before = (0, place + 1) if up else (nz - 1, place - 1)

                @pl.when(z == at)
                def _():
                    if at != first:
                        self.arrive(place, up, self.acc.at[place])
                    elif 0 <= before <= nz - 1:
                        self.along(before, up).wait_send()
                    self.along(place, up).start()

    def final(self, total):
        z, nz = self.z, self.nz
        total[...] = self.acc[z].astype(F32)

        @pl.when(z > 0)
        def _():
            self.arrive(z, True, total)

        @pl.when(z < nz - 1)
        def _():
            self.arrive(z, False, total, nz)

    def end(self):
        for place in range(self.nz):
            self.to_side(place).wait_send()
        for place in range(self.nz):
            last = self.nz - 1
            self_up = jnp.logical_and(self.z < place, jnp.logical_or(self.z > 0, place == 1))
            self_down = jnp.logical_and(
                self.z > place, jnp.logical_or(self.z < last, place == last - 1)
            )
            pl.when(self_up)(self.along(place, True).wait_send)
            pl.when(self_down)(self.along(place, False).wait_send)


class SquareReduce:
    def __init__(self, nf, parts, landed, total, sems, inner=False, shift=0):
        self.nf, self.parts, self.landed, self.total = nf, parts, landed, total
        self.send, self.got = sems
        self.inner, self.shift = inner, shift
        self.half = total.shape[0] // 2

    def part(self, f, at):
        if self.inner:
            return self.parts.at[at, f]
        return self.parts.at[lax.rem(f + self.nf - self.shift, self.nf), at]

    @staticmethod
    def landing(nf, shape):
        blocks, rows, cols = shape
        return (6, blocks // 2, rows, cols) if nf == 4 else (nf, blocks, rows, cols)

    def copy(self, n, src, to):
        return push(src, self.landed.at[n], self.send.at[n], self.got.at[n], {"fsdp": to})

    def way(self, h):
        me, fx, fy = square_partners()
        first, second = (fx, fy) if h == 0 else (fy, fx)
        return me, first, second, pl.ds(h * self.half, self.half)

    def firsts(self, h):
        me, first, second, at = self.way(h)
        return (
            self.copy(3 * h, self.part(3 - me, at), first),
            self.copy(3 * h + 1, self.part(first, at), first),
        )

    def second_(self, h):
        _, _, second, _ = self.way(h)
        return self.copy(3 * h + 2, self.landed.at[3 * h], second)

    def others(self):
        me = lax.axis_index("fsdp")
        tos = [lax.rem(me + j, self.nf) for j in range(1, self.nf)]
        every = pl.ds(0, self.total.shape[0])
        return [self.copy(j + 1, self.part(to, every), to) for j, to in enumerate(tos)]

    def begin(self):
        if self.nf == 4:
            for i in range(2):
                for h in range(2):
                    self.firsts(h)[i].start()
        else:
            for out in self.others():
                out.start()

    def add(self, into, other):
        for b in range(into.shape[0]):
            add_rows(into.at[b], other.at[b], min(16, into.shape[1]))

    def step(self):
        if self.nf == 4:
            for h in range(2):
                _, _, second, at = self.way(h)
                self.firsts(h)[0].wait_recv()
                self.add(self.landed.at[3 * h], self.part(second, at))
                self.second_(h).start()

    def final(self, h):
        me = lax.axis_index("fsdp")
        at = pl.ds(h * self.half, self.half)
        if self.nf == 4:
            self.firsts(h)[1].wait_recv()
            into = self.total.at[at]
            into[...] = self.part(me, at)[...]
            self.add(into, self.landed.at[3 * h + 1])
            self.second_(h).wait_recv()
            self.add(into, self.landed.at[3 * h + 2])
        else:
            into = self.total.at[at]
            into[...] = self.part(me, at)[...]
            for j, out in enumerate(self.others()):
                if h == 0:
                    out.wait_recv()
                self.add(into, self.landed.at[j + 1, at])

    def end(self):
        if self.nf == 4:
            for h in range(2):
                for out in (*self.firsts(h), self.second_(h)):
                    out.wait_send()
        else:
            for out in self.others():
                out.wait_send()


class Deal:
    def __init__(self, nc, parts, pieces, sems, here):
        self.nc, self.parts, self.pieces = nc, parts, pieces
        self.send, self.got, self.here = sems[0], sems[1], here
        self.me = lax.axis_index("ctx")

    def to(self, c):
        return push(
            self.parts.at[c], self.pieces.at[self.me], self.send.at[c], self.got.at[self.me], {"ctx": c}
        )

    def stay(self):
        return pltpu.make_async_copy(self.parts.at[self.me], self.pieces.at[self.me], self.here)

    def start(self, h):
        half = self.nc // 2
        for j in range(half):
            c = h * half + lax.rem(self.me + j, half)
            pl.when(c != self.me)(self.to(c).start)

            @pl.when(c == self.me)
            def _():
                self.stay().start()

    def wait(self):
        self.stay().wait()
        for c in range(self.nc):

            @pl.when(c != self.me)
            def _():
                push(
                    self.parts.at[c], self.pieces.at[c], self.send.at[c], self.got.at[c], {"ctx": c}
                ).wait()


def back_kernel(
    nc, nf, cw, span, lengths, hidden, cot, gain, scales, conv_par, heads_par, chan_par, pick,
    normed_in, cot_in, main_in, tail_in, gated_in, proj_in, gg_in, mixed_in, states_in, branch_in,
    out, d_hidden, grad_in, grad_out, dconv_w, dconv_b, dgain, dheads_out, dnorm_gain,
    normed_t, cot_v, main_v, tail_v, gated_t, proj, gg, mixed, states,
    dnormed, gout, gate_parts, x_parts, acc, landed, total,
    gout_landed, gout_sum, gate_landed, gate_sum, x_landed, x_sum, gate_pieces, x_pieces, gout_mine,
    window, ahead, state_grad, dconv, dheads, dchan,
    small, small_held, small_sum, small_all, gains, gains_held, gains_sum, gains_all,
    load_sems, cot_sems, main_sems, line_sems, way_sems, square_sems, deal_sems, small_sems, route_sems,
    here, line_free, branch_sem,
):
    nz, _, _ = line_of(nc)
    me_c, me_f = lax.axis_index("ctx"), lax.axis_index("fsdp")
    wide, apart = cw // span, DI // span
    cc, ends = cw + 2 * N_STATE, tail_v.shape[1]
    seqs, length = proj.shape[1], proj.shape[2]
    chunks = mixed.shape[0]
    slots = nc * seqs * length

    found = [({"ctx": lax.rem(me_c + j, nc)}, None) for j in range(1, nc)]
    found += [({"fsdp": lax.rem(me_f + j, nf)}, None) for j in range(1, nf)]
    if span > 1:
        turn = lax.rem(me_c // 2, nf)
        lead, place = lax.rem(me_f + nf - turn, nf) * nc + me_c, me_c * nf + me_f
        target = {"ctx": lead // nf, "fsdp": lax.rem(lead, nf)}
        origin = lax.rem(place, nc)
        source = {"ctx": origin, "fsdp": lax.rem(place // nc + lax.rem(origin // 2, nf), nf)}
        away = lead != place
        found += [(target, away), (source, away)]
    met = greet(found)

    loads = []
    branch_load = pltpu.make_async_copy(branch_in, dnormed, branch_sem)
    branch_load.start()
    for i, (src, dst) in enumerate((
        (proj_in, proj), (mixed_in, mixed), (gg_in, gg), (gated_in, gated_t), (normed_in, normed_t),
        (states_in, states),
    )):
        copy = pltpu.make_async_copy(src, dst, load_sems.at[i])
        copy.start()
        loads.append(copy)

    quarter = cot_v.shape[3]

    def cot_part(i):
        return pltpu.make_async_copy(
            cot_in.at[:, :, pl.ds(pl.multiple_of(i * quarter, LANES), quarter)],
            cot_v.at[lax.rem(i, 2)], cot_sems.at[lax.rem(i, 2)],
        )

    def weights_part(f):
        slot = lax.rem(f, 2)
        return (
            pltpu.make_async_copy(main_in.at[f], main_v.at[slot], main_sems.at[0, slot]),
            pltpu.make_async_copy(tail_in.at[f], tail_v.at[slot], main_sems.at[1, slot]),
        )

    def start_weights(f):
        for copy in weights_part(f):
            copy.start()

    for i in range(2):
        cot_part(i).start()
    every_line = [
        LineReduce(
            nc, dnormed.at[i % seqs], acc.at[i % seqs], landed.at[i % seqs],
            (line_sems.at[i, 0], line_sems.at[i, 1], way_sems.at[i, 0], way_sems.at[i, 1]),
        )
        for i in range(2 * seqs)
    ]
    out_lines, lines = every_line[:seqs], every_line[seqs:]
    neighbours = [
        ({"ctx": me_c + 1 - 2 * lax.rem(me_c, 2)}, None),
        ({"ctx": me_c + 2}, me_c + 2 < nc),
        ({"ctx": me_c - 2}, me_c - 2 >= 0),
    ]

    def put_out(s):
        rows = pl.ds(s * length, length)
        out_lines[s].final(total.at[rows])
        out[rows] = (total[rows] + hidden[rows].astype(F32)).astype(BF16)
        out_lines[s].end()
        freed.append(signal_all(line_free.at[s], neighbours))

    freed = []
    square = lambda i, *refs, **how: SquareReduce(
        nf, *refs, (square_sems.at[i, 0], square_sems.at[i, 1]), **how
    )
    gout_square = square(0, gout, gout_landed, gout_sum, shift=turn if span > 1 else 0)
    gate_square = square(1, gate_parts, gate_landed, gate_sum, inner=True)
    x_square = square(2, x_parts, x_landed, x_sum, inner=True)
    gate_deal = Deal(nc, gate_sum, gate_pieces, (deal_sems.at[0, 0], deal_sems.at[0, 1]), here.at[0])
    x_deal = Deal(nc, x_sum, x_pieces, (deal_sems.at[1, 0], deal_sems.at[1, 1]), here.at[1])
    pair = lambda i: (small_sems.at[i, 0], small_sems.at[i, 1])
    smalls = (
        Exchange("fsdp", nf, small, small_held, pair(0)),
        Exchange("ctx", nc, small_sum, small_all, pair(1)),
    )
    gain_sums = (
        Exchange("fsdp", nf, gains, gains_held, pair(2)),
        Exchange("ctx", nc, gains_sum, gains_all, pair(3)),
    )

    for ref in (window, ahead, state_grad, dconv, dheads, dchan, small):
        ref[...] = jnp.zeros_like(ref)
    branch_load.wait()
    met()
    for line in out_lines:
        line.begin()
    for copy in loads[:3]:
        copy.wait()
    for chunk in range(chunks):
        for s in range(seqs):
            gate_chunk(cw, chunk, s, proj, scales, chan_par, gg, mixed, dchan)

    def out_acts(s):
        return [out_lines[s].merge] + [lambda i=i: out_lines[s].step(i) for i in range(nz - 1)]

    first, second = (out_acts(s) for s in (0, seqs - 1))
    first.pop(0)()
    first.pop(0)() if first else None

    loads[3].wait()

    def gout_part(i, _):
        cot_part(i).wait()
        size = min(quarter, 256)
        for j in range(quarter // size):
            cots = cot_v[lax.rem(i, 2), :, :, j * size : (j + 1) * size].reshape(slots, size)
            at = pl.ds(pl.multiple_of(i * quarter + j * size, LANES), size)
            gout[:, :, :, at] = (
                dot(gated_t[...], cots).reshape(gout.shape[:3] + (size,)).astype(BF16)
            )
        pl.when(i + 2 < D // quarter)(lambda: cot_part(i + 2).start())
        return 0

    lax.fori_loop(0, D // quarter, gout_part, 0)
    gout_square.begin()
    first.pop(0)() if first else None
    if seqs > 1:
        second.pop(0)()
        second.pop(0)() if second else None
    loads[4].wait()

    def in_tile(parts, base, shift):
        def body(start, size):
            grads = proj[:, :, :, pl.ds(base + start, size)].reshape(slots, size)
            parts[:, :, :, pl.ds(shift + start, size)] = (
                dot(normed_t[...], grads).reshape(parts.shape[:3] + (size,)).astype(BF16)
            )

        return body

    column_tiles(cw, in_tile(gate_parts, 0, 0))
    gate_square.begin()
    while first:
        first.pop(0)()
    for copy in loads[5:]:
        copy.wait()

    if span > 1:
        route = push(gout_sum, gout_mine, route_sems.at[0], route_sems.at[1], target)
        stay = lambda: pltpu.make_async_copy(gout_sum, gout_mine, here.at[2])

    def finish_gout():
        for h in range(2):
            gout_square.final(h)
        if span > 1:
            pl.when(away)(route.start)
            pl.when(jnp.logical_not(away))(lambda: stay().start())

    def finish_gate():
        for h in range(2):
            gate_square.final(h)
            gate_deal.start(h)

    depth = main_v.shape[2]
    narrow = min(depth, 256)

    def normed_part(s):
        def body(f, _):
            for copy in weights_part(f):
                copy.wait()
            for j in range(depth // narrow):
                here = pl.ds(j * narrow, narrow)
                grads = proj[:, s].reshape(nc * length, proj.shape[3])
                sums = dot(grads[:, : 2 * cw], main_v[lax.rem(f, 2), :, here])
                sums = sums + dot(grads[:, 2 * cw :], tail_v[lax.rem(f, 2), :, here])
                at = pl.ds(pl.multiple_of(f * depth + j * narrow, LANES), narrow)
                dnormed[s, :, :, at] = sums.astype(BF16).reshape(nc, length, narrow)
            pl.when(f + 2 < nf)(lambda: start_weights(f + 2))
            return 0

        lax.fori_loop(0, nf, body, 0)

    def line_acts(line):
        return [line.merge] + [lambda i=i: line.step(i) for i in range(nz - 1)]

    later = [lambda: put_out(0), gout_square.step, gate_square.step, finish_gout]
    if seqs > 1:
        later = second[:1] + later[:1] + second[1:] + later[1:2]
    for s in range(seqs):
        for f in range(min(2, nf)):
            start_weights(f)
        for i in range(chunks):
            backward_chunk(
                cw, chunks - 1 - i, s, lengths, proj, pick, conv_par, heads_par, chan_par, gg, mixed,
                states, dconv, dheads, dchan, window, ahead, state_grad,
            )
            if later:
                later.pop(0)()
        if s == seqs - 1:
            column_tiles(cw, in_tile(x_parts, cw, 0))
            column_tiles(ends, in_tile(x_parts, 2 * cw, cw), ends)
            x_square.begin()
        while later and not (s < len(freed)):
            later.pop(0)()
        normed_part(s)
        freed[s]()
        lines[s].begin()
        if s < seqs - 1:
            acts = line_acts(lines[s])
            later += acts[:2] + [
                lambda: (put_out(1), gate_square.step()), *acts[2:3], finish_gout, *acts[3:], finish_gate
            ]

    for act in later:
        act()

    dskip = dot_exact(jnp.broadcast_to(dchan[0:1, :], (8, cw)), head_sum_matrix(cw))[0:1, :]
    row = 0
    for k in range(CONV_K + 1):
        for j in range(cc // LANES):
            small[row : row + 1, :] = dconv[k : k + 1, j * LANES : (j + 1) * LANES]
            row += 1
    for j in range(cw // LANES):
        small[row : row + 1, :] = dchan[1:2, j * LANES : (j + 1) * LANES]
        row += 1
    small[row : row + 1, :] = dheads[0:1, :]
    small[row + 1 : row + 2, :] = dheads[1:2, :]
    small[row + 2 : row + 3, :] = dskip
    smalls[0].begin()
    acts = line_acts(lines[-1])
    acts.pop(0)()
    acts.pop(0)() if acts else None
    smalls[0].wait()
    small_sum[...] = smalls[0].total()
    smalls[1].begin()
    acts.pop(0)() if acts else None
    x_square.step()
    for act in acts:
        act()
    for s in range(seqs):
        lines[s].final(total.at[pl.ds(s * length, length)])
    dnorm = jnp.zeros((1, D), F32)

    def norm_back(i, dnorm):
        at = pl.ds(pl.multiple_of(i * 16, 16), 16)
        src = hidden[at].astype(F32)
        dn = total[at]
        scale = lax.rsqrt(jnp.mean(src * src, axis=1, keepdims=True) + EPS)
        h = dn * gain[...]
        pull = jnp.mean(h * src, axis=1, keepdims=True) * scale * scale
        d_hidden[at] = scale * (h - src * pull) + cot[at].astype(F32)
        return dnorm + jnp.sum(dn * src * scale, axis=0, keepdims=True)

    dnorm = lax.fori_loop(0, hidden.shape[0] // 16, norm_back, dnorm)
    for j in range(D // LANES):
        gains[j : j + 1, :] = dnorm[:, j * LANES : (j + 1) * LANES]
    gain_sums[0].begin()
    for h in range(2):
        x_square.final(h)
        x_deal.start(h)
    gain_sums[0].wait()
    gains_sum[...] = gain_sums[0].total()
    gain_sums[1].begin()

    def ordered(pieces, base):
        for c in range(nc):
            for i in range(span):
                to = base + i * apart + c * wide
                grad_in[:, to : to + wide] = pieces[c, :, i * wide : (i + 1) * wide].astype(F32)

    gate_deal.wait()
    ordered(gate_pieces, 0)
    if span > 1:

        @pl.when(away)
        def _():
            route.wait_recv()
            route.wait_send()

        @pl.when(jnp.logical_not(away))
        def _():
            stay().wait()

        grad_out[...] = gout_mine[...].reshape(grad_out.shape).astype(F32)
    else:
        grad_out[...] = gout_sum[...].astype(F32).reshape(grad_out.shape)
    smalls[1].wait()
    groups = cc // LANES
    for k in range(CONV_K + 1):
        to_ref, to_row = (dconv_w, k) if k < CONV_K else (dconv_b, 0)
        for c in range(nc):
            for j in range(cw // LANES):
                i, inside = j * LANES // wide, j * LANES % wide
                to = i * apart + c * wide + inside
                to_ref[to_row : to_row + 1, to : to + LANES] = small_all[
                    c, k * groups + j : k * groups + j + 1, :
                ]
        for j in range(cw // LANES, groups):
            shared = small_all[0, k * groups + j : k * groups + j + 1, :]
            for c in range(1, nc):
                shared = shared + small_all[c, k * groups + j : k * groups + j + 1, :]
            to = DI + j * LANES - cw
            to_ref[to_row : to_row + 1, to : to + LANES] = shared
    first = (CONV_K + 1) * groups
    by_head = jnp.zeros((8, HEADS), F32)
    for c in range(nc):
        for j in range(cw // LANES):
            i, inside = j * LANES // wide, j * LANES % wide
            to = i * apart + c * wide + inside
            dgain[:, to : to + LANES] = small_all[c, first + j : first + j + 1, :]
        rows = small_all[c, first + cw // LANES : first + cw // LANES + 8, :]
        by_head = by_head + lax.dot_general(
            rows, head_pick(cw, span, c), (((1,), (1,)), ((), ())), precision=EXACT,
            preferred_element_type=F32,
        )
    dheads_out[...] = by_head
    gain_sums[1].wait()
    summed = gain_sums[1].total()
    for j in range(D // LANES):
        dnorm_gain[:, j * LANES : (j + 1) * LANES] = summed[j : j + 1, :]
    for line in lines:
        line.end()
    gout_square.end()
    gate_square.end()
    x_square.end()
    x_deal.wait()
    ordered(x_pieces, DI)
    shared = x_pieces[0, :, cw:].astype(F32)
    for c in range(1, nc):
        shared = shared + x_pieces[c, :, cw:].astype(F32)
    grad_in[:, 2 * DI :] = shared


def call_back(nc, nf, cw, span, lengths, hidden, cot, gain, *front):
    bigs, params = front[:10], front[10:]
    proj, mixed = bigs[5], bigs[7]
    _, seqs, length, cols = proj.shape
    nz, mine = nc // 2, seqs * length
    slots, q = nc * mine, mixed.shape[2]
    cc, ends, rows = cw + 2 * N_STATE, cols - 2 * cw, D // (nc * nf)
    vmem = pl.BlockSpec(memory_space=pltpu.VMEM)
    anywhere = pl.BlockSpec(memory_space=pl.ANY)
    dma = pltpu.SemaphoreType.DMA
    landing = SquareReduce.landing
    gout = (2, cw // nf // 2, D)
    gate, x = (nc, rows, cw), (nc, rows, cw + ends)
    count = (CONV_K + 1) * (cc // LANES) + cw // LANES + 3
    small = (-(-(count + 5) // 8) * 8, LANES)
    gains = (D // LANES, LANES)
    places = max(nf, 6)
    return pl.pallas_call(
        functools.partial(back_kernel, nc, nf, cw, span),
        in_specs=[pl.BlockSpec(memory_space=pltpu.SMEM)] + [vmem] * 8 + [anywhere] * 10,
        out_specs=[vmem] * 9,
        out_shape=[
            jax.ShapeDtypeStruct((mine, D), BF16),
            jax.ShapeDtypeStruct((mine, D), F32),
            jax.ShapeDtypeStruct((rows, 2 * DI + ends), F32),
            jax.ShapeDtypeStruct((cw // nf, D), F32),
            jax.ShapeDtypeStruct((CONV_K, CH), F32),
            jax.ShapeDtypeStruct((1, CH), F32),
            jax.ShapeDtypeStruct((1, DI), F32),
            jax.ShapeDtypeStruct((8, HEADS), F32),
            jax.ShapeDtypeStruct((1, D), F32),
        ],
        scratch_shapes=[
            pltpu.VMEM(bigs[0].shape, BF16),
            pltpu.VMEM((2, nc, mine, 256), BF16),
            pltpu.VMEM((2,) + bigs[2].shape[1:], BF16),
            pltpu.VMEM((2,) + bigs[3].shape[1:], BF16),
        ]
        + [pltpu.VMEM(a.shape, a.dtype) for a in bigs[4:9]]
        + [
            pltpu.VMEM((seqs, nc, length, D), BF16),
            pltpu.VMEM((nf,) + gout, BF16),
            pltpu.VMEM((nc, nf, rows, cw), BF16),
            pltpu.VMEM((nc, nf, rows, cw + ends), BF16),
            pltpu.VMEM((seqs, nz, length, D), BF16),
            pltpu.VMEM((seqs, nz + 1, length, D), BF16),
            pltpu.VMEM((mine, D), F32),
            pltpu.VMEM(landing(nf, gout), BF16),
            pltpu.VMEM(gout, BF16),
            pltpu.VMEM(landing(nf, gate), BF16),
            pltpu.VMEM(gate, BF16),
            pltpu.VMEM(landing(nf, x), BF16),
            pltpu.VMEM(x, BF16),
            pltpu.VMEM(gate, BF16),
            pltpu.VMEM(x, BF16),
            pltpu.VMEM(gout, BF16),
            pltpu.VMEM((seqs, q + 8, cc), F32),
            pltpu.VMEM((seqs, q + 8, cc), F32),
            pltpu.VMEM((seqs, N_STATE, cw), F32),
            pltpu.VMEM((8, cc), F32),
            pltpu.VMEM((8, LANES), F32),
            pltpu.VMEM((8, cw), F32),
            pltpu.VMEM(small, F32),
            pltpu.VMEM((nf,) + small, F32),
            pltpu.VMEM(small, F32),
            pltpu.VMEM((nc,) + small, F32),
            pltpu.VMEM(gains, F32),
            pltpu.VMEM((nf,) + gains, F32),
            pltpu.VMEM(gains, F32),
            pltpu.VMEM((nc,) + gains, F32),
            dma((6,)),
            dma((2,)),
            dma((2, 2)),
            dma((2 * seqs, 2, nz)),
            dma((2 * seqs, 2, 2, nz)),
            dma((3, 2, places)),
            dma((2, 2, nc)),
            dma((4, 2, max(nc, nf))),
            dma((2,)),
            dma((3,)),
            pltpu.SemaphoreType.REGULAR((seqs,)),
            pltpu.SemaphoreType.DMA,
        ],
        compiler_params=pltpu.CompilerParams(
            collective_id=1, has_side_effects=True, vmem_limit_bytes=VMEM_LIMIT
        ),
        cost_estimate=pl.CostEstimate(
            flops=120_000_000_000, bytes_accessed=200_000_000, transcendentals=0
        ),
        name="back",
    )(lengths, hidden, cot, gain, *params, *bigs)


def finish_kernel(*refs):
    ins, outs, held, sems = refs[:8], refs[8:18], refs[18:26], refs[26]
    copies = [
        pltpu.make_async_copy(src, dst, sems.at[i]) for i, (src, dst) in enumerate(zip(ins, held))
    ]
    for copy in copies:
        copy.start()
    for copy in copies:
        copy.wait()
    for i in range(4):
        outs[i][...] = held[i][...]
    dconv_b, dgain, dheads, dnorm = held[4:]
    outs[4][...] = dconv_b[0]
    for i in range(3):
        outs[5 + i][...] = dheads[i]
    outs[8][...] = dgain[0]
    outs[9][...] = dnorm[0]


def call_finish(*results):
    shapes = [a.shape for a in results[:4]]
    shapes += [(CH,), (HEADS,), (HEADS,), (HEADS,), (DI,), (D,)]
    anywhere, vmem = pl.BlockSpec(memory_space=pl.ANY), pl.BlockSpec(memory_space=pltpu.VMEM)
    return pl.pallas_call(
        finish_kernel,
        in_specs=[anywhere] * 8,
        out_specs=[vmem] * 10,
        out_shape=[jax.ShapeDtypeStruct(a, F32) for a in shapes],
        scratch_shapes=[pltpu.VMEM(a.shape, F32) for a in results] + [pltpu.SemaphoreType.DMA((8,))],
        compiler_params=pltpu.CompilerParams(vmem_limit_bytes=VMEM_LIMIT),
        name="finish",
    )(*results)


def local(
    hidden,
    cotangent,
    lengths,
    norm_gain,
    input_weight,
    conv_w,
    conv_b,
    dt_bias,
    a_log,
    d_skip,
    gate_gain,
    output_weight,
):
    nc, nf = lax.axis_size("ctx"), lax.axis_size("fsdp")
    mb_count, seq_rows, length = hidden.shape[0], hidden.shape[1], hidden.shape[2]
    seqs = mb_count * seq_rows
    mine = seqs * length
    cw = DI // nc

    span = nf if (DI // nf // nc) % LANES == 0 else 1
    own = hidden.reshape(mine, D)
    cot = cotangent.reshape(mine, D)
    heads_in = jnp.pad(jnp.stack([dt_bias, a_log, d_skip]), ((0, 5), (0, 0)))
    seq_lengths = lengths.reshape(seqs)
    front = call_front(
        nc, nf, cw, span, seq_lengths, own, cot, input_weight.T, output_weight,
        norm_gain[None], conv_w, conv_b[None], heads_in, gate_gain[None],
    )
    out, *results = call_back(nc, nf, cw, span, seq_lengths, own, cot, norm_gain[None], *front)
    d_hidden, grad_in, grad_out, dconv_w, dconv_b, dbias, dalog, dskip, dgain, dnorm = call_finish(
        *results
    )
    shape = hidden.shape
    return (
        out.reshape(shape),
        d_hidden.reshape(shape),
        dnorm,
        grad_in,
        dconv_w,
        dconv_b,
        dbias,
        dalog,
        dskip,
        dgain,
        grad_out,
    )


def solution(mesh):
    tokens, rows, every = P(None, "fsdp", "ctx", None), P("fsdp", None), P()
    spread = P(("ctx", "fsdp"), None)
    in_specs = (
        tokens, tokens, P(None, "fsdp"), every, rows, every, every, every, every, every, every, rows,
    )
    out_specs = (
        tokens, tokens, every, spread, every, every, every, every, every, every, spread,
    )
    return jax.shard_map(local, mesh=mesh, in_specs=in_specs, out_specs=out_specs, check_vma=False)
```

profile of v0, /device:TPU:7, one launch (start us, length us, event | category | flops | bytes accessed | tf_op | source)
XLA Modules:
  0.0 258.4 jit_solution(8094643961356225222)
XLA Ops:
  0.6 1.3 select_maximum_fusion.heads_in
  1.9 1.3 broadcast_in_dim.11.conv_b
  3.3 91.9 %front.1 = (bf16[2048,1024]{1,0:T(8,128)(2,1)}, bf16[8,128,2048]{2,1,0:T(8,128)(2,1)}, bf16[4,1024,512]{2,1,0:T(8,128)(2,1)}, bf16[4,320,512]{2,1,0:T(8,128)(2,1...) custom-call(s32[2]{0:T(128)} %bitcast.24, ...), custom_call_target="tpu_custom_call" | custom-call | tf_op jit(solution)/shard_map/front/pallas_call | solution.py:828
  95.2 157.5 %back.1 = (bf16[128,2048]{1,0:T(8,128)(2,1)}, f32[128,2048]{1,0:T(8,128)}, f32[64,8512]{1,0:T(8,128)}, f32[128,2048]{1,0:T(8,128)}, f32[4,4352]{1,0:T(4,128)}, /...) custom-call(s32[2]{0:T(128)} %bitcast.25, bf16[128,2048]{1,0:T(8,128)(2,1)} %bitcast.17, ...), custom_call_target="tpu_custom_call" | custom-call | flops 120000004096 | bytes 200000000 | tf_op jit(solution)/shard_map/back/pallas_call | solution.py:1426
  252.7 0.0 copy-start
  252.7 4.6 %finish.1 = (f32[128,2048]{1,0:T(8,128)}, f32[64,8512]{1,0:T(8,128)}, f32[128,2048]{1,0:T(8,128)}, f32[4,4352]{1,0:T(4,128)}, f32[4352]{0:T(1024)}, /*index=5*/f...) custom-call(f32[128,2048]{1,0:T(8,128)} %get-tuple-element.61.refs_0_, ...), custom_call_target="tpu_custom_call" | custom-call | tf_op jit(solution)/shard_map/finish/pallas_call | solution.py:1525
  257.3 0.0 copy-done
  257.3 0.8 copy.26
Async XLA Ops:
  252.7 4.6 %copy-start = (bf16[128,2048]{1,0:T(8,128)(2,1)S(1)}, bf16[128,2048]{1,0:T(8,128)(2,1)}, u32[]{:S(2)}) copy-start(bf16[128,2048]{1,0:T(8,128)(2,1)} %get-tuple-element.60) | copy-start | bytes 1572868
where the time goes:
time: 261 us; the launch traced here: 258 us
  Pallas kernels  254 us (97%)
    pallas_call x1, Pallas kernels, call_back(): pl.pallas_call(functools.partial(back_kernel, nc, nf, cw, span), in_specs...  157 us
    pallas_call x1, Pallas kernels, call_front(): pl.pallas_call(functools.partial(front_kernel, nc, nf, cw, span), in_spec...  91.9 us

commit v1 on v0

--- a/solution.py
+++ b/solution.py
@@ -1258,9 +1258,10 @@
     def line_acts(line):
         return [line.merge] + [lambda i=i: line.step(i) for i in range(nz - 1)]
 
-    later = [lambda: put_out(0), gout_square.step, gate_square.step, finish_gout]
-    if seqs > 1:
-        later = second[:1] + later[:1] + second[1:] + later[1:2]
+    later = [
+        second[:1], [gout_square.step], [lambda: put_out(0)] + second[1:2],
+        [finish_gout] + second[2:],
+    ]
     for s in range(seqs):
         for f in range(min(2, nf)):
             start_weights(f)
@@ -1270,24 +1271,28 @@
                 states, dconv, dheads, dchan, window, ahead, state_grad,
             )
             if later:
-                later.pop(0)()
+                for act in later.pop(0):
+                    act()
         if s == seqs - 1:
             column_tiles(cw, in_tile(x_parts, cw, 0))
             column_tiles(ends, in_tile(x_parts, 2 * cw, cw), ends)
             x_square.begin()
-        while later and not (s < len(freed)):
-            later.pop(0)()
         normed_part(s)
         freed[s]()
         lines[s].begin()
         if s < seqs - 1:
             acts = line_acts(lines[s])
-            later += acts[:2] + [
-                lambda: (put_out(1), gate_square.step()), *acts[2:3], finish_gout, *acts[3:], finish_gate
+            for left in later:
+                for act in left:
+                    act()
+            later = [
+                acts[:2], [lambda: put_out(seqs - 1), gate_square.step], acts[2:3],
+                acts[3:] + [finish_gate],
             ]
 
-    for act in later:
-        act()
+    for left in later:
+        for act in left:
+            act()
 
     dskip = dot_exact(jnp.broadcast_to(dchan[0:1, :], (8, cw)), head_sum_matrix(cw))[0:1, :]
     row = 0

time: 261 us -> 252 us (0.966)
  the two profiles are of different devices: /device:TPU:7 before, /device:TPU:1 now
where the time goes in v1:
time: 252 us; the launch traced here: 249 us
  Pallas kernels  244 us (97%)
    pallas_call x1, Pallas kernels, call_back(): pl.pallas_call(functools.partial(back_kernel, nc, nf, cw, span), in_specs...  146 us
    pallas_call x1, Pallas kernels, call_front(): pl.pallas_call(functools.partial(front_kernel, nc, nf, cw, span), in_spec...  93.7 us

profile of v1, /device:TPU:1, one launch (start us, length us, event | category | flops | bytes accessed | tf_op | source)
XLA Modules:
  0.0 248.7 jit_solution(11870622177015824220)
XLA Ops:
  0.6 1.3 select_maximum_fusion.heads_in
  1.9 1.3 broadcast_in_dim.11.conv_b
  3.3 93.7 %front.1 = (bf16[2048,1024]{1,0:T(8,128)(2,1)}, bf16[8,128,2048]{2,1,0:T(8,128)(2,1)}, bf16[4,1024,512]{2,1,0:T(8,128)(2,1)}, bf16[4,320,512]{2,1,0:T(8,128)(2,1...) custom-call(s32[2]{0:T(128)} %bitcast.24, ...), custom_call_target="tpu_custom_call" | custom-call | tf_op jit(solution)/shard_map/front/pallas_call | solution.py:828
  97.0 146.0 %back.1 = (bf16[128,2048]{1,0:T(8,128)(2,1)}, f32[128,2048]{1,0:T(8,128)}, f32[64,8512]{1,0:T(8,128)}, f32[128,2048]{1,0:T(8,128)}, f32[4,4352]{1,0:T(4,128)}, /...) custom-call(s32[2]{0:T(128)} %bitcast.25, bf16[128,2048]{1,0:T(8,128)(2,1)} %bitcast.17, ...), custom_call_target="tpu_custom_call" | custom-call | flops 120000004096 | bytes 200000000 | tf_op jit(solution)/shard_map/back/pallas_call | solution.py:1431
  243.0 0.0 copy-start
  243.0 4.6 %finish.1 = (f32[128,2048]{1,0:T(8,128)}, f32[64,8512]{1,0:T(8,128)}, f32[128,2048]{1,0:T(8,128)}, f32[4,4352]{1,0:T(4,128)}, f32[4352]{0:T(1024)}, /*index=5*/f...) custom-call(f32[128,2048]{1,0:T(8,128)} %get-tuple-element.61.refs_0_, ...), custom_call_target="tpu_custom_call" | custom-call | tf_op jit(solution)/shard_map/finish/pallas_call | solution.py:1530
  247.6 0.0 copy-done
  247.6 0.8 copy.26
Async XLA Ops:
  243.0 4.6 %copy-start = (bf16[128,2048]{1,0:T(8,128)(2,1)S(1)}, bf16[128,2048]{1,0:T(8,128)(2,1)}, u32[]{:S(2)}) copy-start(bf16[128,2048]{1,0:T(8,128)(2,1)} %get-tuple-element.60) | copy-start | bytes 1572868
